TPU v7x, 256 devices: a whole 4x4x8 slice. The times are simulated.
256 devices in a mesh: item: 32 (over x, z), cent: 8 (over y, core).
Axes of the slice: x: 4, y: 4, z: 8, core: 2. Of those that a mesh axis runs over, the one named last changes fastest.
Arguments:
- vectors: float32 [32768, 256], P('item'), may hold values from -15 to 15, as said below
- centroids: float32 [32768, 256], P('cent'), may hold values from -15 to 15, as said below
Outputs:
- refined: float32 [32768, 256], P('cent')
- log_partition: float32 [32768], P('item')
Inputs may be any that keep to these rules, and one draw needn't show every extreme that they name: Entries of order one; a few vectors lie on or near centroids, with large norms. Entries of order one or less; a few centroids are larger.
All inputs are finite; a program needn't handle non-finite values.
Results may differ from a plain program's by a relative error of at most 0.0001.
Values sent between devices are 32-bit elements; how exact they have to be, the bound alone decides.
A program may use at most 128 MiB of HBM per device.

v0:
```python
import jax
import jax.numpy as jnp
from jax import lax
from jax.sharding import PartitionSpec as P

BOLTZMANN_SCALE = 8.0
PRIOR = 2.0


def local(vectors, centroids):
    center_energy = jnp.sum(centroids * centroids, axis=1)
    inner_pairings = lax.dot_general(
        vectors,
        centroids,
        (((1,), (1,)), ((), ())),
        precision=lax.Precision.HIGHEST,
        preferred_element_type=jnp.float32,
    )
    cluster_affinity_scores = (2.0 * inner_pairings - center_energy[None, :]) / BOLTZMANN_SCALE
    local_max = jnp.max(cluster_affinity_scores, axis=1)
    row_max = lax.pmax(local_max, "cent")
    row_sum = lax.psum(jnp.sum(jnp.exp(cluster_affinity_scores - row_max[:, None]), axis=1), "cent")
    log_partition = row_max + jnp.log(row_sum)
    probs = jnp.exp(cluster_affinity_scores - log_partition[:, None])
    numer = lax.dot_general(
        probs,
        vectors,
        (((0,), (0,)), ((), ())),
        precision=lax.Precision.HIGHEST,
        preferred_element_type=jnp.float32,
    )
    weight = jnp.sum(probs, axis=0)
    numer_all, weight_all = lax.psum((numer, weight), "item")
    refined = (numer_all + PRIOR * centroids) / (weight_all[:, None] + PRIOR)
    return (refined, log_partition)


def solution(mesh):
    return jax.shard_map(
        local,
        mesh=mesh,
        in_specs=(P("item", None), P("cent", None)),
        out_specs=(P("cent", None), P("item")),
        check_vma=False,
    )
```

profile of v0, /device:TPU:2, one launch (start us, length us, event | category | flops | bytes accessed | tf_op | source)
XLA Modules:
  0.0 271.3 jit_solution(6471339606315500323)
XLA Ops:
  7.2 0.0 copy-start
  7.2 0.0 all-reduce.2.cloned.1.call-start
  7.2 2.9 %multiply_reduce_fusion = f32[4096]{0:T(1024)S(1)} fusion(f32[4096,256]{1,0:T(8,128)} %param.3), kind=kLoop, calls=%fused_computation.7 | loop fusion | flops 2093056 | bytes 4210688 | tf_op jit(solution)/shard_map/reduce_sum | solution.py:11
  10.1 0.0 copy-done
  10.1 19.0 %fusion.3 = (f32[1024]{0:T(1024)S(1)}, f32[1024,4096]{1,0:T(8,128)}) fusion(f32[4096]{0:T(1024)S(1)} %multiply_reduce_fusion, f32[1024,256]{1,0:T(8,128)S(1)} %copy-done, f32[4096,256]{1,0:T(8,128)} %param.3), kind=kOutput, calls=%fused_computation.10 | convolution fusion | flops 12901678080 | bytes 22040576 | tf_op jit(solution)/shard_map/dot_general | solution.py:12
  29.1 14.8 %pmax.7 = f32[1024]{0:T(1024)S(1)} all-reduce(f32[1024]{0:T(1024)S(1)} %get-tuple-element.2), channel_id=1, replica_groups=mesh['item'=32,'cent'=8] {'cent'}, use_global_device_ids=true, to_apply=%region_2.0 | all-reduce | flops 1024 | bytes 8192 | tf_op jit(solution)/shard_map/pmax | solution.py:21
  43.9 8.1 %exponential_reduce_fusion = f32[1024]{0:T(1024)S(1)} fusion(f32[1024,4096]{1,0:T(8,128)} %get-tuple-element.3, f32[1024]{0:T(1024)S(1)} %pmax.7), kind=kLoop, calls=%fused_computation.1 | loop fusion | flops 8387584 | bytes 16785408 | tf_op jit(solution)/shard_map/reduce_sum | solution.py:22
  52.0 12.6 %psum.21 = f32[1024]{0:T(1024)S(1)} all-reduce(f32[1024]{0:T(1024)S(1)} %exponential_reduce_fusion), channel_id=1, replica_groups=mesh['item'=32,'cent'=8] {'cent'}, use_global_device_ids=true, to_apply=%region_4.0 | all-reduce | flops 1024 | bytes 8192 | tf_op jit(solution)/shard_map/psum | solution.py:22
  64.6 0.0 copy-start.1
  64.7 30.9 %fusion.1 = f32[4096,256]{1,0:T(8,128)} fusion(f32[1024,256]{1,0:T(8,128)S(1)} %copy-done, f32[1024,4096]{1,0:T(8,128)} %get-tuple-element.3, f32[1024]{0:T(1024)S(1)} %log_add_fusion), kind=kOutput, calls=%fused_computation.4 | convolution fusion | flops 12889096192 | bytes 22024192 | tf_op jit(solution)/shard_map/dot_general | solution.py:25
  95.6 0.0 all-reduce.2.cloned.1.call-update
  95.6 8.3 %fusion = f32[4096]{0:T(1024)S(1)} fusion(f32[1024,4096]{1,0:T(8,128)} %get-tuple-element.3, f32[1024]{0:T(1024)S(1)} %log_add_fusion), kind=kLoop, calls=%fused_computation.3 | loop fusion | flops 8384512 | bytes 16797696 | tf_op jit(solution)/shard_map/reduce_sum | solution.py:32
  103.8 0.0 copy-done.1
  103.8 134.0 %psum.23 = f32[4096]{0:T(1024)S(1)} all-reduce(f32[4096]{0:T(1024)S(1)} %fusion), channel_id=1, replica_groups=mesh['item'=32,'cent'=8] {'item'}, use_global_device_ids=true, to_apply=%region_7.0 | all-reduce | flops 4096 | bytes 32768 | tf_op jit(solution)/shard_map/psum | solution.py:33
  237.9 21.4 %all-reduce.2.cloned.1.call-done = f32[4096,256]{1,0:T(8,128)} async-done(((f32[4096,256]{1,0:T(8,128)}), f32[4096,256]{1,0:T(8,128)}) %all-reduce.2.cloned.1.call-update) | async-done | bytes 4194320 | tf_op jit(solution)/shard_map/psum | solution.py:33
  259.3 5.1 %add_divide_fusion = f32[4096,256]{1,0:T(8,128)} fusion(f32[4096,256]{1,0:T(8,128)} %all-reduce.2.cloned.1.call-done, f32[4096,256]{1,0:T(8,128)} %param.3, f32[4096]{0:T(1024)S(1)} %broadcast_add_fusion), kind=kLoop, calls=%fused_computation.6 | loop fusion | flops 3145728 | bytes 12599296 | tf_op jit(solution)/shard_map/div | solution.py:34
  (2 shorter events, 0.0 us)
Async XLA Ops:
  7.2 3.0 %copy-start = (f32[1024,256]{1,0:T(8,128)S(1)}, f32[1024,256]{1,0:T(8,128)}, u32[]{:S(2)}) copy-start(f32[1024,256]{1,0:T(8,128)} %param.2) | copy-start | bytes 3145732
  7.2 252.1 %all-reduce.2.cloned.1.call-start = ((), (), s32[]{:S(2)}) async-start(), calls=%async_computation | async-start | bytes 8388608 | tf_op jit(solution)/shard_map/psum | solution.py:33
  64.6 39.2 %copy-start.1 = (f32[1024]{0:T(1024)}, f32[1024]{0:T(1024)S(1)}, u32[]{:S(2)}) copy-start(f32[1024]{0:T(1024)S(1)} %log_add_fusion) | copy-start | bytes 12292
Sparse Core Ops, SparseCore 0:
  95.7 163.5 all-reduce.1
where the time goes:
time: 273 us; the launch traced here: 271 us
  blocking collectives  161 us (59%)
  matrix products  49.9 us (18%)
  other arithmetic  24.4 us (9%)
  waiting for transfers between devices  21.4 us (8%)
  between operations  14.1 us (5%)
    psum x1, blocking collectives, local(): numer_all, weight_all = lax.psum((numer, weight), 'item')  134 us
    dot_general x1, matrix products, local(): lax.dot_general(probs, vectors, (((0,), (0,)), ((), ())), precision=lax.P...  30.9 us
    psum x1, waiting for transfers between devices, local(): numer_all, weight_all = lax.psum((numer, weight), 'item')  21.4 us
    dot_general x1, matrix products, local(): lax.dot_general(vectors, centroids, (((1,), (1,)), ((), ())), precision=l...  19 us
    pmax x1, blocking collectives, local(): row_max = lax.pmax(local_max, 'cent')  14.8 us
    psum x1, blocking collectives, local(): lax.psum(jnp.sum(jnp.exp(cluster_affinity_scores - row_max[:, None]), axi...  12.6 us
    reduce_sum x1, other arithmetic, local(): weight = jnp.sum(probs, axis=0)  8.26 us
    reduce_sum x1, other arithmetic, local(): jnp.sum(jnp.exp(cluster_affinity_scores - row_max[:, None]), axis=1)  8.09 us
  transfers between devices with their start and end apart: 1, of which 1 were waited for; matrix products, arithmetic and copies ran while one was open for 3% of the time, Pallas kernels for 0%

commit v1 on v0

v1 whole, which is shorter than its diff:
```python
import functools
import math

import jax
import jax.numpy as jnp
from jax import lax
from jax.experimental import pallas as pl
from jax.experimental.pallas import tpu as pltpu
from jax.sharding import PartitionSpec as P

MESH = pl.DeviceIdType.MESH
BOLTZMANN_SCALE = 8.0
PRIOR = 2.0
LOG2E = math.log2(math.e)
LN2 = math.log(2.0)
XSCALE = 2.0 * LOG2E / BOLTZMANN_SCALE

NX, NZ, NC = 4, 8, 8
D = 256
N = 1024
KP = 4096
RA, RB = 80, 48
CA, CB = NZ * RA, NX * RB
B0 = NX * CA
TILE = 512
NT = KP // TILE
G = 64

STAT = 0
W1 = STAT + 7
W2 = W1 + 3
A1 = W2 + 7
A2 = A1 + 16
AZ = A2 + 16
BZ = AZ + 8
BX = BZ + 8
GAZ = BX + 4
GA1 = GAZ + 8
GA2 = GA1 + 16
GBX = GA2 + 16
GBZ = GBX + 4
NSEM = GBZ + 8

ORDER_RS = (4, 3, -3, 2, -2, 1, -1, 0)
ORDER_AG = (0, -1, 1, -2, 2, -3, 3, 4)


def dot(a, b):
    return jnp.dot(a, b, preferred_element_type=jnp.float32)


def split(v):
    hi = v.astype(jnp.bfloat16)
    lo = (v - hi.astype(jnp.float32)).astype(jnp.bfloat16)
    return hi, lo


def kernel(
    x_hbm, c_hbm, out, lse_out,
    xbuf, cbuf, xh, xl, xht, xlt, e_buf, m_buf, s_buf, f_buf, stat, numer, w8,
    wown, rw1, w2s, rw2, ra1, ra2, raz0, raz, rbz0, rbz, rbx0, rbx, den,
    ss, rs, lsem,
):
    item = lax.axis_index("item")
    cent = lax.axis_index("cent")
    x, z = item // NZ, lax.rem(item, NZ)

    def mod(v, n):
        return lax.rem(v + 2 * n, n)

    def at_x(d):
        return {"item": mod(x + d, NX) * NZ + z}

    def at_z(d):
        return {"item": x * NZ + mod(z + d, NZ)}

    def at_c(d):
        return {"cent": mod(cent + d, NC)}

    pending = []

    def copy(src, dst, k, dev):
        return pltpu.make_async_remote_copy(
            src_ref=src, dst_ref=dst, send_sem=ss.at[k], recv_sem=rs.at[k],
            device_id=dev, device_id_type=MESH,
        )

    def send(src, dst, k, dev):
        c = copy(src, dst, k, dev)
        c.start()
        pending.append(c)

    def got(region, k):
        copy(region, region, k, at_x(1)).wait_recv()

    x_load = pltpu.make_async_copy(x_hbm, xbuf, lsem.at[NT])
    x_load.start()

    def c_load(t):
        rows = pl.ds(t * TILE, TILE)
        return pltpu.make_async_copy(c_hbm.at[rows], cbuf.at[rows], lsem.at[t])

    for t in range(NT):
        c_load(t).start()

    barrier = pltpu.get_barrier_semaphore()
    for d in range(1, NX):
        pl.semaphore_signal(barrier, inc=1, device_id=at_x(d), device_id_type=MESH)
    for d in range(1, NZ):
        pl.semaphore_signal(barrier, inc=1, device_id=at_z(d), device_id_type=MESH)
    for d in range(1, NC):
        pl.semaphore_signal(barrier, inc=1, device_id=at_c(d), device_id_type=MESH)

    x_load.wait()
    for j in range(N // 256):
        rows = pl.ds(j * 256, 256)
        v = xbuf[rows, :] * XSCALE
        hi, lo = split(v)
        xh[rows, :] = hi
        xl[rows, :] = lo
        hi, lo = split(v.T)
        xht[:, rows] = hi
        xlt[:, rows] = lo

    def tile_a(t, _):
        c_load(t).wait()
        rows = pl.ds(pl.multiple_of(t * TILE, TILE), TILE)
        c = cbuf[rows, :]
        csq = jnp.sum(c * c, axis=1, keepdims=True) * (LOG2E / BOLTZMANN_SCALE)
        ch, cl = split(c)
        for j in range(N // 256):
            cols = pl.ds(j * 256, 256)
            b = xht[:, cols]
            l = dot(ch, b) + dot(cl, b) + dot(ch, xlt[:, cols]) - csq
            l = l.reshape(TILE // 8, 8, 256)
            m = jnp.max(l, axis=0)
            e = jnp.exp2(l - m[None])
            s = jnp.sum(e, axis=0)
            e_buf[rows, cols] = e.reshape(TILE, 256)
            m_buf[t, :, cols] = m
            s_buf[t, :, cols] = s
        return 0

    lax.fori_loop(0, NT, tile_a, 0)

    mm = m_buf[...]
    m_loc = jnp.max(jnp.max(mm, axis=0), axis=0, keepdims=True)
    s_loc = jnp.sum(
        jnp.sum(s_buf[...] * jnp.exp2(mm - m_loc[None]), axis=0), axis=0, keepdims=True
    )
    stat[cent] = m_loc + jnp.log(s_loc) * LOG2E
    pl.semaphore_wait(barrier, (NX - 1) + (NZ - 1) + (NC - 1))
    for d in range(1, NC):
        send(stat.at[cent], stat.at[cent], STAT + d - 1, at_c(d))
    for d in range(1, NC):
        got(stat.at[mod(cent - d, NC)], STAT + d - 1)
    parts = stat[...]
    top = jnp.max(parts, axis=0)
    total = jnp.log(jnp.sum(jnp.exp2(parts - top[None]), axis=0))
    lse_out[...] = top * LN2 + total
    lse2 = top + total * LOG2E
    f_buf[...] = jnp.exp2(mm - lse2[None])

    def block_b(r0, rows_n):
        rows = pl.ds(pl.multiple_of(r0, G), rows_n)
        hs, ls, ws = [], [], []
        for g in range(rows_n // G):
            start = pl.multiple_of(r0 + g * G, G)
            p = e_buf[pl.ds(start, G), :].reshape(G // 8, 8, N) * f_buf[start // TILE][None]
            p = p.reshape(G, N)
            w = p[:, 0:128]
            for q in range(1, N // 128):
                w = w + p[:, q * 128 : (q + 1) * 128]
            w8[pl.ds(start, G), :] = w
            hi, lo = split(p)
            hs.append(hi)
            ls.append(lo)
        hi = jnp.concatenate(hs, axis=0)
        lo = jnp.concatenate(ls, axis=0)
        numer[rows, :] = dot(hi, xh[...]) + dot(lo, xh[...]) + dot(hi, xl[...])

    def chunk_a(d):
        base = mod(x + d, NX) * CA

        def body(i, _):
            block_b(base + i * (CA // 2), CA // 2)
            return 0

        lax.fori_loop(0, 2, body, 0)

    def chunks_b(d0, n):
        def body(i, _):
            block_b(B0 + mod(z + d0 + i, NZ) * CB, CB)
            return 0

        lax.fori_loop(0, n, body, 0)

    def rows_a(dx, dz, off=0, n=RA):
        return pl.ds(pl.multiple_of(mod(x + dx, NX) * CA + mod(z + dz, NZ) * RA + off, 8), n)

    def rows_b(dz, dx, off=0, n=RB):
        return pl.ds(pl.multiple_of(B0 + mod(z + dz, NZ) * CB + mod(x + dx, NX) * RB + off, 8), n)

    def chunk_rows_b(dz, off=0, n=CB):
        return pl.ds(pl.multiple_of(B0 + mod(z + dz, NZ) * CB + off, 8), n)

    def add(rows, ref):
        numer[rows, :] += ref[...]

    HA, HB, HC = RA // 2, RB // 2, CB // 2

    chunk_a(2)
    for i, o in enumerate(ORDER_RS):
        send(numer.at[rows_a(2, o, 0, HA)], ra1.at[0, i], A1 + i, at_x(1))
        send(numer.at[rows_a(2, o, HA, HA)], ra1.at[1, i], A1 + 8 + i, at_x(-1))
    chunks_b(4, 1)
    send(numer.at[chunk_rows_b(4, 0, HC)], rbz0.at[0], BZ, at_z(1))
    send(numer.at[chunk_rows_b(4, HC, HC)], rbz0.at[1], BZ + 4, at_z(-1))
    chunks_b(3, 1)
    chunks_b(-3, 1)
    chunk_a(1)

    def bz_step(k):
        if k == 1:
            got(rbz0.at[0], BZ)
            add(chunk_rows_b(3, 0, HC), rbz0.at[0])
        else:
            got(rbz.at[k - 2, 0], BZ + k - 1)
            add(chunk_rows_b(4 - k), rbz.at[k - 2, 0])
        send(numer.at[chunk_rows_b(4 - k)], rbz.at[k - 1, 0], BZ + k, at_z(1))
        if k == 1:
            got(rbz0.at[1], BZ + 4)
            add(chunk_rows_b(-3, HC, HC), rbz0.at[1])
        else:
            got(rbz.at[k - 2, 1], BZ + 4 + k - 1)
            add(chunk_rows_b(k - 4), rbz.at[k - 2, 1])
        send(numer.at[chunk_rows_b(k - 4)], rbz.at[k - 1, 1], BZ + 4 + k, at_z(-1))

    bz_step(1)
    chunk_a(-1)
    chunks_b(-2, 5)
    chunk_a(0)

    def owner_weights(i, _):
        xd, zd = i // NZ, lax.rem(i, NZ)
        a = w8[pl.ds(pl.multiple_of(xd * CA + zd * RA, 8), RA), :]
        b = w8[pl.ds(pl.multiple_of(B0 + zd * CB + xd * RB, 8), RB), :]
        t = jnp.concatenate([a, b], axis=0).T
        wown[xd, pl.ds(zd, 1), :] = jnp.sum(t, axis=0, keepdims=True)
        return 0

    lax.fori_loop(0, NX * NZ, owner_weights, 0)
    for d in range(1, NX):
        send(wown.at[mod(x + d, NX)], rw1.at[d - 1], W1 + d - 1, at_x(d))

    def a1_step(i):
        o = ORDER_RS[i]
        got(ra1.at[0, i], A1 + i)
        add(rows_a(1, o, 0, HA), ra1.at[0, i])
        send(numer.at[rows_a(1, o)], ra2.at[0, i], A2 + i, at_x(1))
        got(ra1.at[1, i], A1 + 8 + i)
        add(rows_a(-1, o, HA, HA), ra1.at[1, i])
        send(numer.at[rows_a(-1, o)], ra2.at[1, i], A2 + 8 + i, at_x(-1))

    def a2_step(i):
        o = ORDER_RS[i]
        got(ra2.at[0, i], A2 + i)
        got(ra2.at[1, i], A2 + 8 + i)
        numer[rows_a(0, o), :] += ra2[0, i] + ra2[1, i]

    for i in range(4):
        a1_step(i)
    bz_step(2)
    for i in range(4, 8):
        a1_step(i)

    for d in range(1, NX):
        got(rw1.at[d - 1], W1 + d - 1)
    w = wown[x] + rw1[0] + rw1[1] + rw1[2]
    for s in range(NZ):
        w2s[s] = w[s : s + 1, :]
    for d in range(1, NZ):
        send(w2s.at[mod(z + d, NZ)], rw2.at[d - 1], W2 + d - 1, at_z(d))

    bz_step(3)
    a2_step(0)
    send(numer.at[rows_a(0, 4, 0, HA)], raz0.at[0], AZ, at_z(1))
    send(numer.at[rows_a(0, 4, HA, HA)], raz0.at[1], AZ + 4, at_z(-1))

    def az_step(k):
        if k == 1:
            got(raz0.at[0], AZ)
            add(rows_a(0, 3, 0, HA), raz0.at[0])
        else:
            got(raz.at[k - 2, 0], AZ + k - 1)
            add(rows_a(0, 4 - k), raz.at[k - 2, 0])
        send(numer.at[rows_a(0, 4 - k)], raz.at[k - 1, 0], AZ + k, at_z(1))
        if k == 1:
            got(raz0.at[1], AZ + 4)
            add(rows_a(0, -3, HA, HA), raz0.at[1])
        else:
            got(raz.at[k - 2, 1], AZ + 4 + k - 1)
            add(rows_a(0, k - 4), raz.at[k - 2, 1])
        send(numer.at[rows_a(0, k - 4)], raz.at[k - 1, 1], AZ + 4 + k, at_z(-1))

    a2_step(1)
    a2_step(2)
    az_step(1)

    got(rbz.at[2, 0], BZ + 3)
    got(rbz.at[2, 1], BZ + 7)
    numer[chunk_rows_b(0), :] += rbz[2, 0] + rbz[2, 1]
    send(numer.at[rows_b(0, 2, 0, HB)], rbx0.at[0], BX, at_x(1))
    send(numer.at[rows_b(0, 2, HB, HB)], rbx0.at[1], BX + 2, at_x(-1))
    a2_step(3)
    a2_step(4)
    az_step(2)
    got(rbx0.at[0], BX)
    add(rows_b(0, 1, 0, HB), rbx0.at[0])
    send(numer.at[rows_b(0, 1)], rbx.at[0], BX + 1, at_x(1))
    got(rbx0.at[1], BX + 2)
    add(rows_b(0, -1, HB, HB), rbx0.at[1])
    send(numer.at[rows_b(0, -1)], rbx.at[1], BX + 3, at_x(-1))

    w = w2s[z]
    for d in range(1, NZ):
        got(rw2.at[d - 1], W2 + d - 1)
        w = w + rw2[d - 1]
    den[...] = jnp.broadcast_to(w, (RA + RB, RA + RB)).T + PRIOR

    def finish(rows, total_rows, den_rows):
        q = den[den_rows, :]
        q = jnp.concatenate([q, q], axis=1)
        out[rows, :] = (total_rows * (1.0 / XSCALE) + PRIOR * cbuf[rows, :]) / q

    a2_step(5)
    a2_step(6)
    az_step(3)
    got(rbx.at[0], BX + 1)
    got(rbx.at[1], BX + 3)
    own_b = rows_b(0, 0)
    finish(own_b, numer[own_b, :] + rbx[0] + rbx[1], pl.ds(RA, RB))
    send(out.at[own_b], out.at[own_b], GBX, at_x(1))
    send(out.at[own_b], out.at[own_b], GBX + 2, at_x(-1))

    a2_step(7)
    got(raz.at[2, 0], AZ + 3)
    got(raz.at[2, 1], AZ + 7)
    own_a = rows_a(0, 0)
    finish(own_a, numer[own_a, :] + raz[2, 0] + raz[2, 1], pl.ds(0, RA))

    def gaz_send(k):
        if k < 3:
            r, l = rows_a(0, -k), rows_a(0, k)
        else:
            r, l = rows_a(0, -3, 0, HA), rows_a(0, 3, HA, HA)
        send(out.at[r], out.at[r], GAZ + k, at_z(1))
        send(out.at[l], out.at[l], GAZ + 4 + k, at_z(-1))

    def gaz_got(k):
        if k < 3:
            r, l = rows_a(0, -1 - k), rows_a(0, 1 + k)
        else:
            r, l = rows_a(0, 4, 0, HA), rows_a(0, 4, HA, HA)
        got(out.at[r], GAZ + k)
        got(out.at[l], GAZ + 4 + k)

    def ga1_send(i):
        r = rows_a(0, ORDER_AG[i])
        send(out.at[r], out.at[r], GA1 + i, at_x(1))
        send(out.at[r], out.at[r], GA1 + 8 + i, at_x(-1))

    def ga2_step(i):
        o = ORDER_AG[i]
        got(out.at[rows_a(-1, o)], GA1 + i)
        r = rows_a(-1, o, 0, HA)
        send(out.at[r], out.at[r], GA2 + i, at_x(1))
        got(out.at[rows_a(1, o)], GA1 + 8 + i)
        l = rows_a(1, o, HA, HA)
        send(out.at[l], out.at[l], GA2 + 8 + i, at_x(-1))

    def ga2_got(i):
        o = ORDER_AG[i]
        got(out.at[rows_a(2, o, 0, HA)], GA2 + i)
        got(out.at[rows_a(2, o, HA, HA)], GA2 + 8 + i)

    def gbz_send(k):
        if k < 3:
            r, l = chunk_rows_b(-k), chunk_rows_b(k)
        else:
            r, l = chunk_rows_b(-3, 0, HC), chunk_rows_b(3, HC, HC)
        send(out.at[r], out.at[r], GBZ + k, at_z(1))
        send(out.at[l], out.at[l], GBZ + 4 + k, at_z(-1))

    def gbz_got(k):
        if k < 3:
            r, l = chunk_rows_b(-1 - k), chunk_rows_b(1 + k)
        else:
            r, l = chunk_rows_b(4, 0, HC), chunk_rows_b(4, HC, HC)
        got(out.at[r], GBZ + k)
        got(out.at[l], GBZ + 4 + k)

    gaz_send(0)
    ga1_send(0)
    got(out.at[rows_b(0, -1)], GBX)
    r = rows_b(0, -1, 0, HB)
    send(out.at[r], out.at[r], GBX + 1, at_x(1))
    got(out.at[rows_b(0, 1)], GBX + 2)
    l = rows_b(0, 1, HB, HB)
    send(out.at[l], out.at[l], GBX + 3, at_x(-1))
    gaz_got(0)
    gaz_send(1)
    ga1_send(1)
    ga1_send(2)
    got(out.at[rows_b(0, 2, 0, HB)], GBX + 1)
    got(out.at[rows_b(0, 2, HB, HB)], GBX + 3)
    gbz_send(0)
    gaz_got(1)
    gaz_send(2)
    ga1_send(3)
    ga1_send(4)
    ga2_step(0)
    gaz_got(2)
    gaz_send(3)
    ga1_send(5)
    ga1_send(6)
    gbz_got(0)
    gbz_send(1)
    gaz_got(3)
    ga1_send(7)
    ga2_step(1)
    ga2_step(2)
    gbz_got(1)
    gbz_send(2)
    ga2_step(3)
    ga2_step(4)
    gbz_got(2)
    gbz_send(3)
    ga2_step(5)
    ga2_step(6)
    ga2_step(7)
    gbz_got(3)
    for i in range(8):
        ga2_got(i)
    for c in pending:
        c.wait_send()


def local(vectors, centroids):
    f32, bf16 = jnp.float32, jnp.bfloat16
    V = pltpu.VMEM
    refined, lse = pl.pallas_call(
        kernel,
        out_shape=(
            jax.ShapeDtypeStruct((KP, D), f32),
            jax.ShapeDtypeStruct((1, N), f32),
        ),
        in_specs=[pl.BlockSpec(memory_space=pl.ANY)] * 2,
        out_specs=[pl.BlockSpec(memory_space=pltpu.VMEM)] * 2,
        scratch_shapes=[
            V((N, D), f32), V((KP, D), f32),
            V((N, D), bf16), V((N, D), bf16), V((D, N), bf16), V((D, N), bf16),
            V((KP, N), f32), V((NT, 8, N), f32), V((NT, 8, N), f32), V((NT, 8, N), f32),
            V((NC, 1, N), f32), V((KP, D), f32), V((KP, 128), f32),
            V((NX, NZ, 128), f32), V((NX - 1, NZ, 128), f32),
            V((NZ, 1, 128), f32), V((NZ - 1, 1, 128), f32),
            V((2, 8, RA // 2, D), f32), V((2, 8, RA, D), f32),
            V((2, RA // 2, D), f32), V((3, 2, RA, D), f32),
            V((2, CB // 2, D), f32), V((3, 2, CB, D), f32),
            V((2, RB // 2, D), f32), V((2, RB, D), f32),
            V((RA + RB, RA + RB), f32),
            pltpu.SemaphoreType.DMA((NSEM,)), pltpu.SemaphoreType.DMA((NSEM,)),
            pltpu.SemaphoreType.DMA((NT + 1,)),
        ],
        compiler_params=pltpu.CompilerParams(
            collective_id=0, has_side_effects=True, vmem_limit_bytes=58 * 1024 * 1024
        ),
    )(vectors, centroids)
    return refined, lse.reshape(N)


def solution(mesh):
    return jax.shard_map(
        local,
        mesh=mesh,
        in_specs=(P("item", None), P("cent", None)),
        out_specs=(P("cent", None), P("item")),
        check_vma=False,
    )
```

time: 273 us -> 102 us (0.37)
  blocking collectives: 161 us -> 0 us
  Pallas kernels: 0 us -> 95.8 us
  matrix products: 49.9 us -> 0 us
  other arithmetic: 24.4 us -> 0 us
  waiting for transfers between devices: 21.4 us -> 0 us
  between operations: 14.1 us -> 0.65 us
  local copies, waits for them, and re-layouts: 0.02 us -> 5.07 us
    psum x2 -> x0, blocking collectives: 147 us -> none  [the longest x1 134 us: local(): numer_all, weight_all = lax.psum((numer, weight), 'item')]
    pallas_call x0 -> x1, Pallas kernels: none -> 95.8 us  [local(): pl.pallas_call(kernel, out_shape=(jax.ShapeDtypeStruct((KP, D), f32), jax...]
    dot_general x2 -> x0, matrix products: 49.9 us -> none  [the longest x1 30.9 us: local(): lax.dot_general(probs, vectors, (((0,), (0,)), ((), ())), precision=lax.P...]
    psum x1 -> x0, waiting for transfers between devices: 21.4 us -> none  [local(): numer_all, weight_all = lax.psum((numer, weight), 'item')]
    reduce_sum x3 -> x0, other arithmetic: 19.2 us -> none  [the longest x1 8.26 us: local(): weight = jnp.sum(probs, axis=0)]
    pmax x1 -> x0, blocking collectives: 14.8 us -> none  [local(): row_max = lax.pmax(local_max, 'cent')]
    div x1 -> x0, other arithmetic: 5.13 us -> none  [local(): refined = (numer_all + PRIOR * centroids) / (weight_all[:, None] + PRIOR)]
    unnamed x4, local copies, waits for them, and re-layouts: 0.02 us -> 5.07 us
  transfers between devices with their start and end apart: 1 -> 0, of which waited for: 1 -> 0; matrix products, arithmetic and copies ran while one was open for 3% -> 0% of each run, Pallas kernels for 0% -> 0%
where the time goes in v1:
time: 102 us
  Pallas kernels  95.8 us (94%)
  local copies, waits for them, and re-layouts  5.07 us (5%)
    pallas_call x1, Pallas kernels, local(): pl.pallas_call(kernel, out_shape=(jax.ShapeDtypeStruct((KP, D), f32), jax...  95.8 us
    unnamed x4, local copies, waits for them, and re-layouts  5.07 us

profile of v1, /device:TPU:2, one launch (start us, length us, event | category | flops | bytes accessed | tf_op | source)
XLA Modules:
  0.0 101.5 jit_solution(9647308026863151147)
XLA Ops:
  0.6 95.8 %shard_map.41 = (f32[4096,256]{1,0:T(8,128)}, f32[1,1024]{1,0:T(1,128)}) custom-call(f32[1024,256]{1,0:T(8,128)} %x_hbm.1, f32[4096,256]{1,0:T(8,128)} %c_hbm.1), custom_call_target="tpu_custom_call" | custom-call | tf_op jit(solution)/shard_map/pallas_call | solution.py:452
  96.5 0.0 copy-start
  96.5 4.5 %copy.6 = f32[4096,256]{1,0:T(8,128)} copy(f32[4096,256]{1,0:T(8,128)} %get-tuple-element.8) | data formatting | bytes 8388608
  100.9 0.0 copy-done
  100.9 0.6 copy.7
Async XLA Ops:
  96.5 4.5 %copy-start = (f32[1,1024]{1,0:T(1,128)S(1)}, f32[1,1024]{1,0:T(1,128)}, u32[]{:S(2)}) copy-start(f32[1,1024]{1,0:T(1,128)} %get-tuple-element.5) | copy-start | bytes 12292
